TPU v7x, 32 devices: a whole 2x2x4 slice. The times are simulated.
32 devices in a mesh: cells: 8 (over z, x), modes: 4 (over y, core).
Axes of the slice: x: 2, y: 2, z: 4, core: 2. Of those that a mesh axis runs over, the one named last changes fastest.
Arguments:
- pressure: bfloat16 [256, 8192], P('modes', 'cells'), may hold values from -6 to 6
- storage: float32 [8192], P('cells'), may hold values from 0.5 to 2
- coupling: bfloat16 [11, 256, 256], P(None, 'modes'), as said below
- transmissibility: float32 [11, 24576], P(None, 'cells'), as said below
- face_cells: int32 [2, 24576], P(None, 'cells'), may hold values from 0 to 1535, as said below
- send_list: int32 [8, 4, 128], P('cells'), may hold values from -1 to 1023, as said below
Outputs:
- first_image: bfloat16 [256, 8192], P('modes', 'cells')
- second_image: bfloat16 [256, 8192], P('modes', 'cells')
Inputs may be any that keep to these rules, and one draw needn't show every extreme that they name: send_list[p, s] lists distinct owned cells of partition p, in local numbers, wanted by partition p + o_s with o = (-2, ..., -1, 1, ..., 2), followed by -1 padding; lists toward partitions outside the axis hold only -1; in every draw some list toward a lower partition and some list toward a higher partition are full. Face f of partition q joins the owned cell face_cells[0, f] with face_cells[1, f], which is a different owned cell where it is below 1024, else ghost slot s * 128 + g offset by 1024, holding entry g of send_list[q + o_s, 3 - s]; a ghost slot is named only where that entry is not -1, and every such entry is named by exactly one face. Each coupling matrix is symmetric. The first row of transmissibility is positive.
All inputs are finite; a program needn't handle non-finite values.
Results may differ from a plain program's by a relative error of at most 0.0041.
Values may be sent and summed in bfloat16 or wider, within the bound.
A program may use at most 64 MiB of HBM per device.

v0:
```python
import functools

import jax
import jax.numpy as jnp
from jax import lax
from jax.experimental import pallas as pl
from jax.experimental.pallas import tpu as pltpu
from jax.sharding import PartitionSpec as P

MESH = pl.DeviceIdType.MESH
BLOCK = 256
TILE = 512
AHEAD = 2


def onehot(rows, base, index_row, dtype=jnp.bfloat16):
    near = jnp.clip(index_row - base, -1, rows).astype(jnp.float32).astype(jnp.bfloat16)
    iota = lax.broadcasted_iota(jnp.int32, (rows, index_row.shape[1]), 0)
    return iota.astype(jnp.float32).astype(jnp.bfloat16) == near


def kernel(
    parts, groups, pressure, storage_in, coupling_in, trans_in, faces_in, sends_in, first, second,
    storage, coupling, trans, faces, sends,
    wide, ghost_hot, picked_rows, fields, sums, totals, flux, out_w, in_w, out_t, in_t, slot_owner,
    load, near_send, near_recv, far_send, far_recv, pass_send, pass_recv,
    w_send, w_recv, t_send, t_recv,
):
    rows, cells = pressure.shape
    terms = coupling.shape[0]
    face_count = faces.shape[1]
    lists, width = sends.shape[1:]
    ghosts = lists * width
    reach = lists // 2
    offsets = list(range(-reach, 0)) + list(range(1, reach + 1))
    chunks = cells // BLOCK
    part = lax.axis_index("cells")
    group = lax.axis_index("modes")
    partner = group + 1 - 2 * lax.rem(group, 2)
    far = lax.rem(group + 2, 4)
    far_partner = lax.rem(partner + 2, 4)

    def band(member):
        return pl.ds(pl.multiple_of(member * rows, rows), rows)

    mine = band(group)
    one = jnp.ones((), jnp.bfloat16)
    zero = jnp.zeros((), jnp.bfloat16)

    def present(slot):
        return jnp.logical_and(part + offsets[slot] >= 0, part + offsets[slot] < parts)

    def band_copy(app, chunk, member, send_sem, recv_sem, target):
        return pltpu.make_async_remote_copy(
            src_ref=fields.at[app, chunk, band(member)],
            dst_ref=fields.at[app, chunk, band(member)],
            send_sem=send_sem.at[app, chunk],
            recv_sem=recv_sem.at[app, chunk],
            device_id={"modes": target},
            device_id_type=MESH,
        )

    def near_copy(app, chunk, member=group):
        return band_copy(app, chunk, member, near_send, near_recv, partner)

    def far_copy(app, chunk, member=group):
        return band_copy(app, chunk, member, far_send, far_recv, far)

    def pass_copy(app, chunk, member=far):
        return band_copy(app, chunk, member, pass_send, pass_recv, partner)

    def flux_copy(app, slot):
        return pltpu.make_async_remote_copy(
            src_ref=out_w.at[app, slot],
            dst_ref=in_w.at[app, lists - 1 - slot],
            send_sem=w_send.at[app, slot],
            recv_sem=w_recv.at[app, lists - 1 - slot],
            device_id={"cells": part + offsets[slot]},
            device_id_type=MESH,
        )

    def flux_wait(app, slot):
        return pltpu.make_async_remote_copy(
            src_ref=out_w.at[app, lists - 1 - slot],
            dst_ref=in_w.at[app, slot],
            send_sem=w_send.at[app, lists - 1 - slot],
            recv_sem=w_recv.at[app, slot],
            device_id={"cells": part + offsets[slot]},
            device_id_type=MESH,
        )

    def weight_copy(slot):
        return pltpu.make_async_remote_copy(
            src_ref=out_t.at[slot],
            dst_ref=in_t.at[lists - 1 - slot],
            send_sem=t_send.at[slot],
            recv_sem=t_recv.at[lists - 1 - slot],
            device_id={"cells": part + offsets[slot]},
            device_id_type=MESH,
        )

    def weight_wait(slot):
        return pltpu.make_async_remote_copy(
            src_ref=out_t.at[lists - 1 - slot],
            dst_ref=in_t.at[slot],
            send_sem=t_send.at[lists - 1 - slot],
            recv_sem=t_recv.at[slot],
            device_id={"cells": part + offsets[slot]},
            device_id_type=MESH,
        )

    loads = [
        pltpu.make_async_copy(
            pressure.at[:, chunk * BLOCK:(chunk + 1) * BLOCK], fields.at[0, chunk, mine], load.at[chunk]
        )
        for chunk in range(chunks)
    ]
    for index, (source, target) in enumerate(
        ((faces_in, faces), (trans_in, trans), (sends_in, sends), (storage_in, storage),
         (coupling_in, coupling))
    ):
        loads.append(pltpu.make_async_copy(source, target, load.at[chunks + index]))
    for copy in loads:
        copy.start()
    in_w[...] = jnp.zeros_like(in_w)
    in_t[...] = jnp.zeros_like(in_t)
    barrier = pltpu.get_barrier_semaphore()
    for peer in (partner, far):
        pl.semaphore_signal(barrier, inc=1, device_id={"modes": peer}, device_id_type=MESH)
    peers = 2
    for slot in range(lists):
        peers = peers + present(slot).astype(jnp.int32)

        @pl.when(present(slot))
        def _():
            pl.semaphore_signal(
                barrier, inc=1, device_id={"cells": part + offsets[slot]}, device_id_type=MESH
            )
    for chunk in range(chunks):
        loads[chunk].wait()
    pl.semaphore_wait(barrier, peers)
    for chunk in range(chunks):
        far_copy(0, chunk).start()
        near_copy(0, chunk).start()
    for copy in loads[chunks:]:
        copy.wait()

    t = trans[...]
    t_high = t.astype(jnp.bfloat16)
    t_low = (t - t_high.astype(jnp.float32)).astype(jnp.bfloat16)
    picked_rows[...] = jnp.zeros_like(picked_rows)
    picked_rows[0:terms] = t_high
    picked_rows[16:16 + terms] = t_low
    owner = faces[0:1]
    owner_next = owner + 1
    picked_rows[32:33] = (owner_next // 32).astype(jnp.float32).astype(jnp.bfloat16)
    picked_rows[33:34] = (owner_next % 32).astype(jnp.float32).astype(jnp.bfloat16)

    def build_ghost(index, carry):
        at = pl.ds(pl.multiple_of(index * TILE, TILE), TILE)
        other = faces[1:2, at]
        for base in range(0, ghosts, BLOCK):
            hot = onehot(BLOCK, cells + base, other)
            ghost_hot[base:base + BLOCK, at] = jnp.where(hot, one, zero)
        return carry

    lax.fori_loop(0, face_count // TILE, build_ghost, 0)
    found = lax.dot_general(
        picked_rows[...], ghost_hot[...], (((1,), (1,)), ((), ())), preferred_element_type=jnp.float32
    )
    weights = found[0:16] + found[16:32]
    slot_owner[0:1] = (found[32:33] * 32.0 + found[33:34] - 1.0).astype(jnp.int32)
    for slot in range(lists):
        out_t[slot] = weights[:, slot * width:(slot + 1) * width]

        @pl.when(present(slot))
        def _():
            weight_copy(slot).start()

    def build_block(base):
        for slot in range(lists):
            hot = onehot(BLOCK, base, sends[0, slot:slot + 1])
            wide[base:base + BLOCK, slot * width:(slot + 1) * width] = jnp.where(hot, one, zero)

        def build_faces(index, carry):
            at = pl.ds(pl.multiple_of(index * TILE, TILE), TILE)
            to = pl.ds(pl.multiple_of(ghosts + index * TILE, TILE), TILE)
            plus = onehot(BLOCK, base, faces[0:1, at])
            minus = onehot(BLOCK, base, faces[1:2, at])
            wide[base:base + BLOCK, to] = jnp.where(plus, one, jnp.where(minus, -one, zero))
            return carry

        lax.fori_loop(0, face_count // TILE, build_faces, 0)
        hot = onehot(BLOCK, base, slot_owner[0:1])
        wide[base:base + BLOCK, ghosts + face_count:] = jnp.where(hot, -one, zero)

    tiles = [(start, min(TILE, ghosts + face_count - start)) for start in range(0, ghosts + face_count, TILE)]

    def across(app, chunk, start, size):
        rows_of = slice(chunk * BLOCK, (chunk + 1) * BLOCK)
        part_sum = jnp.dot(
            fields[app, chunk], wide[rows_of, start:start + size], preferred_element_type=jnp.float32
        )
        return part_sum if chunk == 0 else sums[:, start:start + size] + part_sum

    def mix(app, start, size, weights):
        column = across(app, chunks - 1, start, size).astype(jnp.bfloat16)
        stacked = coupling[...].reshape(terms * rows, groups * rows)
        mixed = jnp.dot(stacked, column, preferred_element_type=jnp.float32)
        total = mixed[0:rows] * weights[0:1]
        for term in range(1, terms):
            total += mixed[term * rows:(term + 1) * rows] * weights[term:term + 1]
        return total

    for app, target in enumerate((first, second)):
        for chunk in range(chunks + 1):
            if chunk < chunks:
                if app == 0:
                    build_block(chunk * BLOCK)
                far_copy(app, chunk, far).wait_recv()
                pass_copy(app, chunk).start()
            if chunk > 0:
                near_copy(app, chunk - 1, partner).wait_recv()
                pass_copy(app, chunk - 1, far_partner).wait_recv()
                if chunk < chunks:
                    for start, size in tiles:
                        sums[:, start:start + size] = across(app, chunk - 1, start, size)
        if app == 0:
            for slot in range(lists):
                @pl.when(present(slot))
                def _():
                    weight_wait(slot).wait_recv()
        sent_weights = jnp.concatenate([in_t[slot] for slot in range(lists)], axis=1)
        sent = mix(app, 0, ghosts, sent_weights)
        for slot in range(lists):
            out_w[app, slot] = sent[:, slot * width:(slot + 1) * width].astype(jnp.bfloat16)

            @pl.when(present(slot))
            def _():
                flux_copy(app, slot).start()

        for start in range(0, face_count, TILE):
            at = slice(start, start + TILE)
            total = mix(app, ghosts + start, TILE, trans[:, at])
            high = total.astype(jnp.bfloat16)
            flux[0:rows, at] = high
            flux[rows:2 * rows, at] = (total - high.astype(jnp.float32)).astype(jnp.bfloat16)

        def inner(chunk):
            span = slice(chunk * BLOCK, (chunk + 1) * BLOCK)
            spread = lax.dot_general(
                flux[...], wide[span, ghosts:ghosts + face_count], (((1,), (1,)), ((), ())),
                preferred_element_type=jnp.float32,
            )
            image = storage[:, span] * fields[app, chunk, mine, :].astype(jnp.float32)
            return image + spread[0:rows] + spread[rows:2 * rows]

        def finish(chunk, image, arrived):
            span = slice(chunk * BLOCK, (chunk + 1) * BLOCK)
            spread = lax.dot_general(
                arrived, wide[span, ghosts + face_count:], (((1,), (1,)), ((), ())),
                preferred_element_type=jnp.float32,
            )
            image = (image + spread).astype(jnp.bfloat16)
            target[:, span] = image
            if app == 0:
                fields[1, chunk, mine, :] = image
                far_copy(1, chunk).start()
                near_copy(1, chunk).start()

        ahead = min(AHEAD, chunks)
        for chunk in range(ahead):
            totals[:, chunk * BLOCK:(chunk + 1) * BLOCK] = inner(chunk)
        for slot in range(lists):
            @pl.when(present(slot))
            def _():
                flux_wait(app, slot).wait_recv()
        arrived = jnp.concatenate([in_w[app, slot] for slot in range(lists)], axis=1)
        for chunk in range(ahead):
            finish(chunk, totals[:, chunk * BLOCK:(chunk + 1) * BLOCK], arrived)
        for chunk in range(ahead, chunks):
            finish(chunk, inner(chunk), arrived)

    for app in range(2):
        for chunk in range(chunks):
            far_copy(app, chunk).wait_send()
            near_copy(app, chunk).wait_send()
            pass_copy(app, chunk).wait_send()
    for slot in range(lists):
        @pl.when(present(slot))
        def _():
            weight_copy(slot).wait_send()
            for app in range(2):
                flux_copy(app, slot).wait_send()


def local(parts, groups, pressure, storage, coupling, trans, face_cells, send_list):
    assert groups == 4
    rows, cells = pressure.shape
    face_count = face_cells.shape[1]
    lists, width = send_list.shape[1:]
    ghosts = lists * width
    chunks = cells // BLOCK
    bf16 = jnp.bfloat16
    vmem = pl.BlockSpec(memory_space=pltpu.VMEM)
    image = jax.ShapeDtypeStruct((rows, cells), bf16)
    return pl.pallas_call(
        functools.partial(kernel, parts, groups),
        out_shape=(image, image),
        in_specs=[pl.BlockSpec(memory_space=pltpu.HBM)] * 6,
        out_specs=(vmem, vmem),
        scratch_shapes=[
            pltpu.VMEM((1, cells), jnp.float32),
            pltpu.VMEM(coupling.shape, bf16),
            pltpu.VMEM(trans.shape, jnp.float32),
            pltpu.VMEM(face_cells.shape, jnp.int32),
            pltpu.VMEM(send_list.shape, jnp.int32),
            pltpu.VMEM((cells, 2 * ghosts + face_count), bf16),
            pltpu.VMEM((ghosts, face_count), bf16),
            pltpu.VMEM((48, face_count), bf16),
            pltpu.VMEM((2, chunks, groups * rows, BLOCK), bf16),
            pltpu.VMEM((groups * rows, ghosts + face_count), jnp.float32),
            pltpu.VMEM((rows, cells), jnp.float32),
            pltpu.VMEM((2 * rows, face_count), bf16),
            pltpu.VMEM((2, lists, rows, width), bf16),
            pltpu.VMEM((2, lists, rows, width), bf16),
            pltpu.VMEM((lists, 16, width), jnp.float32),
            pltpu.VMEM((lists, 16, width), jnp.float32),
            pltpu.VMEM((8, ghosts), jnp.int32),
            pltpu.SemaphoreType.DMA((chunks + 5,)),
        ]
        + [pltpu.SemaphoreType.DMA((2, chunks))] * 6
        + [pltpu.SemaphoreType.DMA((2, lists))] * 2
        + [pltpu.SemaphoreType.DMA((lists,))] * 2,
        compiler_params=pltpu.CompilerParams(
            collective_id=0, has_side_effects=True, vmem_limit_bytes=63 * 1024 * 1024
        ),
    )(pressure, storage.reshape(1, cells), coupling, trans, face_cells, send_list)


def solution(mesh):
    placed = (
        P("modes", "cells"),
        P("cells"),
        P(None, "modes", None),
        P(None, "cells"),
        P(None, "cells"),
        P("cells", None, None),
    )
    return jax.shard_map(
        functools.partial(local, mesh.shape["cells"], mesh.shape["modes"]),
        mesh=mesh,
        in_specs=placed,
        out_specs=(P("modes", "cells"), P("modes", "cells")),
        check_vma=False,
    )
```

profile of v0, /device:TPU:0, one launch (start us, length us, event | category | flops | bytes accessed | tf_op | source)
XLA Modules:
  0.0 30.5 jit_solution(13898041577665735269)
XLA Ops:
  0.6 27.6 %shard_map.77 = (bf16[64,1024]{1,0:T(8,128)(2,1)}, bf16[64,1024]{1,0:T(8,128)(2,1)}) custom-call(bf16[64,1024]{1,0:T(8,128)(2,1)} %pressure.1, f32[1,1024]{1,0:T(1,128)} %bitcast.1, bf16[11,64,256]{2,1,0:T(8,128)(2,1)} %coupling_in.1, f32[11,3072]{1,0:T(8,128)} %trans_in.1, s32[2,3072]{1,0:T(2,128)} %faces_in.1, s32[1,4,128]{2,1,0:T(4,128)} %sends_in.1), custom_call_target="tpu_custom_call" | custom-call | tf_op jit(solution)/shard_map/pallas_call | solution.py:307
  28.3 0.0 copy-start
  28.3 1.6 %copy.10 = bf16[64,1024]{1,0:T(8,128)(2,1)} copy(bf16[64,1024]{1,0:T(8,128)(2,1)} %get-tuple-element.4) | data formatting | bytes 262144
  29.9 0.0 copy-done
  29.9 0.7 %copy.11 = bf16[64,1024]{1,0:T(8,128)(2,1)} copy(bf16[64,1024]{1,0:T(8,128)(2,1)S(1)} %copy-done) | data formatting | bytes 262144
Async XLA Ops:
  28.3 1.6 %copy-start = (bf16[64,1024]{1,0:T(8,128)(2,1)S(1)}, bf16[64,1024]{1,0:T(8,128)(2,1)}, u32[]{:S(2)}) copy-start(bf16[64,1024]{1,0:T(8,128)(2,1)} %get-tuple-element.5) | copy-start | bytes 393220
where the time goes:
time: 30.7 us; the launch traced here: 30.5 us
  Pallas kernels  27.6 us (90%)
  local copies, waits for them, and re-layouts  2.26 us (7%)
  between operations  0.65 us (2%)
    pallas_call x1, Pallas kernels, local(): pl.pallas_call(functools.partial(kernel, parts, groups), out_shape=(image...  27.6 us
    unnamed x4, local copies, waits for them, and re-layouts  2.26 us

commit v1 on v0

--- a/solution.py
+++ b/solution.py
@@ -294,6 +294,17 @@
                 flux_copy(app, slot).wait_send()
 
 
+def write_out(first_in, second_in, first, second, done):
+    copies = [
+        pltpu.make_async_copy(source, target, done.at[index])
+        for index, (source, target) in enumerate(((first_in, first), (second_in, second)))
+    ]
+    for copy in copies:
+        copy.start()
+    for copy in copies:
+        copy.wait()
+
+
 def local(parts, groups, pressure, storage, coupling, trans, face_cells, send_list):
     assert groups == 4
     rows, cells = pressure.shape
@@ -304,9 +315,9 @@
     bf16 = jnp.bfloat16
     vmem = pl.BlockSpec(memory_space=pltpu.VMEM)
     image = jax.ShapeDtypeStruct((rows, cells), bf16)
-    return pl.pallas_call(
+    images = pl.pallas_call(
         functools.partial(kernel, parts, groups),
-        out_shape=(image, image),
+        out_shape=(pltpu.VMEM((rows, cells), bf16), pltpu.VMEM((rows, cells), bf16)),
         in_specs=[pl.BlockSpec(memory_space=pltpu.HBM)] * 6,
         out_specs=(vmem, vmem),
         scratch_shapes=[
@@ -333,9 +344,18 @@
         + [pltpu.SemaphoreType.DMA((2, lists))] * 2
         + [pltpu.SemaphoreType.DMA((lists,))] * 2,
         compiler_params=pltpu.CompilerParams(
-            collective_id=0, has_side_effects=True, vmem_limit_bytes=63 * 1024 * 1024
+            collective_id=0, has_side_effects=True, vmem_limit_bytes=61 * 1024 * 1024
         ),
     )(pressure, storage.reshape(1, cells), coupling, trans, face_cells, send_list)
+    hbm = pl.BlockSpec(memory_space=pltpu.HBM)
+    return pl.pallas_call(
+        write_out,
+        out_shape=(image, image),
+        in_specs=[vmem] * 2,
+        out_specs=(hbm, hbm),
+        scratch_shapes=[pltpu.SemaphoreType.DMA((2,))],
+        compiler_params=pltpu.CompilerParams(vmem_limit_bytes=1024 * 1024),
+    )(*images)
 
 
 def solution(mesh):

time: 30.7 us -> 28.3 us (0.922)
  local copies, waits for them, and re-layouts: 2.26 us -> 0 us
    unnamed x4 -> x0, local copies, waits for them, and re-layouts: 2.26 us -> none
    pallas_call x1 -> x2, Pallas kernels: 27.6 us -> 27.5 us  [the longest x1 26.8 us: local(): pl.pallas_call(functools.partial(kernel, parts, groups), out_shape=(pltpu...]
where the time goes in v1:
time: 28.3 us; the launch traced here: 28.1 us
  Pallas kernels  27.5 us (97%)
  between operations  0.64 us (2%)
    pallas_call x1, Pallas kernels, local(): pl.pallas_call(functools.partial(kernel, parts, groups), out_shape=(pltpu...  26.8 us
    pallas_call x1, Pallas kernels, local(): pl.pallas_call(write_out, out_shape=(image, image), in_specs=[vmem] * 2,...  0.72 us

profile of v1, /device:TPU:0, one launch (start us, length us, event | category | flops | bytes accessed | tf_op | source)
XLA Modules:
  0.0 28.1 jit_solution(17793062665474040916)
XLA Ops:
  0.6 26.8 %shard_map.77 = (bf16[64,1024]{1,0:T(8,128)(2,1)S(1)}, bf16[64,1024]{1,0:T(8,128)(2,1)S(1)}) custom-call(bf16[64,1024]{1,0:T(8,128)(2,1)} %pressure.1, f32[1,1024]{1,0:T(1,128)} %bitcast.1, bf16[11,64,256]{2,1,0:T(8,128)(2,1)} %coupling_in.1, f32[11,3072]{1,0:T(8,128)} %trans_in.1, s32[2,3072]{1,0:T(2,128)} %faces_in.1, s32[1,4,128]{2,1,0:T(4,128)} %sends_in.1), custom_call_target="tpu_custom_call" | custom-call | tf_op jit(solution)/shard_map/pallas_call | solution.py:318
  27.4 0.7 %shard_map.78 = (bf16[64,1024]{1,0:T(8,128)(2,1)}, bf16[64,1024]{1,0:T(8,128)(2,1)}) custom-call(bf16[64,1024]{1,0:T(8,128)(2,1)S(1)} %get-tuple-element.4.first_in, bf16[64,1024]{1,0:T(8,128)(2,1)S(1)} %get-tuple-element.5.second_in), custom_call_target="tpu_custom_call" | custom-call | tf_op jit(solution)/shard_map/pallas_call | solution.py:351

commit v2 on v1

--- a/solution.py
+++ b/solution.py
@@ -10,7 +10,6 @@
 MESH = pl.DeviceIdType.MESH
 BLOCK = 256
 TILE = 512
-AHEAD = 2
 
 
 def onehot(rows, base, index_row, dtype=jnp.bfloat16):
@@ -21,10 +20,10 @@
 
 def kernel(
     parts, groups, pressure, storage_in, coupling_in, trans_in, faces_in, sends_in, first, second,
-    storage, coupling, trans, faces, sends,
-    wide, ghost_hot, picked_rows, fields, sums, totals, flux, out_w, in_w, out_t, in_t, slot_owner,
+    storage, coupling, trans, faces, sends, pair, turned,
+    wide, tall, ghost_hot, picked_rows, fields, sums, diff, totals, flux, out_w, in_w, out_t, in_t, slot_owner, ghost,
     load, near_send, near_recv, far_send, far_recv, pass_send, pass_recv,
-    w_send, w_recv, t_send, t_recv,
+    w_send, w_recv, t_send, t_recv, pair_send, pair_recv,
 ):
     rows, cells = pressure.shape
     terms = coupling.shape[0]
@@ -69,23 +68,38 @@
     def pass_copy(app, chunk, member=far):
         return band_copy(app, chunk, member, pass_send, pass_recv, partner)
 
-    def flux_copy(app, slot):
-        return pltpu.make_async_remote_copy(
-            src_ref=out_w.at[app, slot],
-            dst_ref=in_w.at[app, lists - 1 - slot],
-            send_sem=w_send.at[app, slot],
-            recv_sem=w_recv.at[app, lists - 1 - slot],
-            device_id={"cells": part + offsets[slot]},
-            device_id_type=MESH,
-        )
-
-    def flux_wait(app, slot):
-        return pltpu.make_async_remote_copy(
-            src_ref=out_w.at[app, lists - 1 - slot],
-            dst_ref=in_w.at[app, slot],
-            send_sem=w_send.at[app, lists - 1 - slot],
-            recv_sem=w_recv.at[app, slot],
-            device_id={"cells": part + offsets[slot]},
+    def flux_peer(side, slot):
+        peer = part + offsets[slot]
+        return {"cells": peer} if side == 0 else {"cells": peer, "modes": far}
+
+    def flux_copy(app, side, slot):
+        return pltpu.make_async_remote_copy(
+            src_ref=out_w.at[app, side, slot],
+            dst_ref=in_w.at[app, side, lists - 1 - slot],
+            send_sem=w_send.at[app, side, slot],
+            recv_sem=w_recv.at[app, side, lists - 1 - slot],
+            device_id=flux_peer(side, slot),
+            device_id_type=MESH,
+        )
+
+    def flux_wait(app, side, slot):
+        return pltpu.make_async_remote_copy(
+            src_ref=out_w.at[app, side, lists - 1 - slot],
+            dst_ref=in_w.at[app, side, slot],
+            send_sem=w_send.at[app, side, lists - 1 - slot],
+            recv_sem=w_recv.at[app, side, slot],
+            device_id=flux_peer(side, slot),
+            device_id_type=MESH,
+        )
+
+    def pair_copy(member):
+        at = pl.ds(pl.multiple_of(lax.rem(member, 2) * rows, rows), rows)
+        return pltpu.make_async_remote_copy(
+            src_ref=pair.at[:, at],
+            dst_ref=pair.at[:, at],
+            send_sem=pair_send.at[0],
+            recv_sem=pair_recv.at[0],
+            device_id={"modes": partner},
             device_id_type=MESH,
         )
 
@@ -117,6 +131,7 @@
     ]
     for index, (source, target) in enumerate(
         ((faces_in, faces), (trans_in, trans), (sends_in, sends), (storage_in, storage),
+         (coupling_in, pair.at[:, pl.ds(pl.multiple_of(lax.rem(group, 2) * rows, rows), rows)]),
          (coupling_in, coupling))
     ):
         loads.append(pltpu.make_async_copy(source, target, load.at[chunks + index]))
@@ -129,20 +144,17 @@
         pl.semaphore_signal(barrier, inc=1, device_id={"modes": peer}, device_id_type=MESH)
     peers = 2
     for slot in range(lists):
-        peers = peers + present(slot).astype(jnp.int32)
+        peers = peers + 2 * present(slot).astype(jnp.int32)
 
         @pl.when(present(slot))
         def _():
             pl.semaphore_signal(
                 barrier, inc=1, device_id={"cells": part + offsets[slot]}, device_id_type=MESH
             )
-    for chunk in range(chunks):
-        loads[chunk].wait()
-    pl.semaphore_wait(barrier, peers)
-    for chunk in range(chunks):
-        far_copy(0, chunk).start()
-        near_copy(0, chunk).start()
-    for copy in loads[chunks:]:
+            pl.semaphore_signal(
+                barrier, inc=1, device_id={"cells": part + offsets[slot], "modes": far}, device_id_type=MESH
+            )
+    for copy in loads:
         copy.wait()
 
     t = trans[...]
@@ -172,10 +184,15 @@
     slot_owner[0:1] = (found[32:33] * 32.0 + found[33:34] - 1.0).astype(jnp.int32)
     for slot in range(lists):
         out_t[slot] = weights[:, slot * width:(slot + 1) * width]
-
+    pl.semaphore_wait(barrier, peers)
+    for chunk in range(chunks):
+        far_copy(0, chunk).start()
+        near_copy(0, chunk).start()
+    for slot in range(lists):
         @pl.when(present(slot))
         def _():
             weight_copy(slot).start()
+    pair_copy(group).start()
 
     def build_block(base):
         for slot in range(lists):
@@ -187,99 +204,117 @@
             to = pl.ds(pl.multiple_of(ghosts + index * TILE, TILE), TILE)
             plus = onehot(BLOCK, base, faces[0:1, at])
             minus = onehot(BLOCK, base, faces[1:2, at])
-            wide[base:base + BLOCK, to] = jnp.where(plus, one, jnp.where(minus, -one, zero))
+            signs = jnp.where(plus, one, jnp.where(minus, -one, zero))
+            wide[base:base + BLOCK, to] = signs
+            tall[at, base:base + BLOCK] = signs.T
             return carry
 
         lax.fori_loop(0, face_count // TILE, build_faces, 0)
         hot = onehot(BLOCK, base, slot_owner[0:1])
-        wide[base:base + BLOCK, ghosts + face_count:] = jnp.where(hot, -one, zero)
-
-    tiles = [(start, min(TILE, ghosts + face_count - start)) for start in range(0, ghosts + face_count, TILE)]
-
-    def across(app, chunk, start, size):
+        tall[face_count:, base:base + BLOCK] = jnp.where(hot, -one, zero).T
+
+
+    half = 2 * rows
+    near_half = pl.ds(pl.multiple_of(lax.div(group, 2) * half, half), half)
+    far_half = pl.ds(pl.multiple_of((1 - lax.div(group, 2)) * half, half), half)
+
+    def differ(app, chunk, members):
         rows_of = slice(chunk * BLOCK, (chunk + 1) * BLOCK)
-        part_sum = jnp.dot(
-            fields[app, chunk], wide[rows_of, start:start + size], preferred_element_type=jnp.float32
-        )
-        return part_sum if chunk == 0 else sums[:, start:start + size] + part_sum
-
-    def mix(app, start, size, weights):
-        column = across(app, chunks - 1, start, size).astype(jnp.bfloat16)
-        stacked = coupling[...].reshape(terms * rows, groups * rows)
+        field = fields[app, chunk, members]
+        for start in range(0, face_count, TILE):
+            at = slice(start, start + TILE)
+            total = jnp.dot(
+                field, wide[rows_of, ghosts + start:ghosts + start + TILE], preferred_element_type=jnp.float32
+            )
+            if chunk > 0:
+                total += sums[:, at]
+            if chunk < chunks - 1:
+                sums[:, at] = total
+            else:
+                diff[members, at] = total.astype(jnp.bfloat16)
+
+    def pick(app):
+        total = jnp.dot(fields[app, 0, near_half], wide[0:BLOCK, 0:ghosts], preferred_element_type=jnp.float32)
+        for chunk in range(1, chunks):
+            total += jnp.dot(
+                fields[app, chunk, near_half], wide[chunk * BLOCK:(chunk + 1) * BLOCK, 0:ghosts],
+                preferred_element_type=jnp.float32,
+            )
+        ghost[...] = total.astype(jnp.bfloat16)
+
+    def mix(stacked, column, weights):
         mixed = jnp.dot(stacked, column, preferred_element_type=jnp.float32)
         total = mixed[0:rows] * weights[0:1]
         for term in range(1, terms):
             total += mixed[term * rows:(term + 1) * rows] * weights[term:term + 1]
         return total
 
+    for chunk in range(chunks):
+        build_block(chunk * BLOCK)
+    pair_copy(partner).wait_recv()
+
+    def turn(term, carry):
+        turned[term] = pair[term].T
+        return carry
+
+    lax.fori_loop(0, terms, turn, 0)
     for app, target in enumerate((first, second)):
-        for chunk in range(chunks + 1):
-            if chunk < chunks:
-                if app == 0:
-                    build_block(chunk * BLOCK)
-                far_copy(app, chunk, far).wait_recv()
-                pass_copy(app, chunk).start()
-            if chunk > 0:
-                near_copy(app, chunk - 1, partner).wait_recv()
-                pass_copy(app, chunk - 1, far_partner).wait_recv()
-                if chunk < chunks:
-                    for start, size in tiles:
-                        sums[:, start:start + size] = across(app, chunk - 1, start, size)
+        for chunk in range(chunks):
+            near_copy(app, chunk, partner).wait_recv()
+        pick(app)
         if app == 0:
             for slot in range(lists):
                 @pl.when(present(slot))
                 def _():
                     weight_wait(slot).wait_recv()
         sent_weights = jnp.concatenate([in_t[slot] for slot in range(lists)], axis=1)
-        sent = mix(app, 0, ghosts, sent_weights)
+        for side, member in enumerate((group, far)):
+            sent = mix(turned[:, band(member)].reshape(terms * rows, half), ghost[...], sent_weights)
+            for slot in range(lists):
+                out_w[app, side, slot] = sent[:, slot * width:(slot + 1) * width].astype(jnp.bfloat16)
         for slot in range(lists):
-            out_w[app, slot] = sent[:, slot * width:(slot + 1) * width].astype(jnp.bfloat16)
-
             @pl.when(present(slot))
             def _():
-                flux_copy(app, slot).start()
-
+                for side in (1, 0):
+                    flux_copy(app, side, slot).start()
+        for chunk in range(chunks):
+            far_copy(app, chunk, far).wait_recv()
+            pass_copy(app, chunk).start()
+            differ(app, chunk, near_half)
+        for chunk in range(chunks):
+            pass_copy(app, chunk, far_partner).wait_recv()
+            differ(app, chunk, far_half)
+
+        stacked = coupling[...].reshape(terms * rows, groups * rows)
         for start in range(0, face_count, TILE):
             at = slice(start, start + TILE)
-            total = mix(app, ghosts + start, TILE, trans[:, at])
+            total = mix(stacked, diff[:, at], trans[:, at])
             high = total.astype(jnp.bfloat16)
             flux[0:rows, at] = high
             flux[rows:2 * rows, at] = (total - high.astype(jnp.float32)).astype(jnp.bfloat16)
 
-        def inner(chunk):
+        for chunk in range(chunks):
             span = slice(chunk * BLOCK, (chunk + 1) * BLOCK)
-            spread = lax.dot_general(
-                flux[...], wide[span, ghosts:ghosts + face_count], (((1,), (1,)), ((), ())),
-                preferred_element_type=jnp.float32,
-            )
+            spread = jnp.dot(flux[...], tall[0:face_count, span], preferred_element_type=jnp.float32)
             image = storage[:, span] * fields[app, chunk, mine, :].astype(jnp.float32)
-            return image + spread[0:rows] + spread[rows:2 * rows]
-
-        def finish(chunk, image, arrived):
+            totals[:, span] = image + spread[0:rows] + spread[rows:2 * rows]
+        for slot in range(lists):
+            @pl.when(present(slot))
+            def _():
+                for side in range(2):
+                    flux_wait(app, side, slot).wait_recv()
+        arrived = jnp.concatenate(
+            [jnp.concatenate([in_w[app, side, slot] for slot in range(lists)], axis=1) for side in range(2)], axis=0
+        )
+        for chunk in range(chunks):
             span = slice(chunk * BLOCK, (chunk + 1) * BLOCK)
-            spread = lax.dot_general(
-                arrived, wide[span, ghosts + face_count:], (((1,), (1,)), ((), ())),
-                preferred_element_type=jnp.float32,
-            )
-            image = (image + spread).astype(jnp.bfloat16)
+            spread = jnp.dot(arrived, tall[face_count:, span], preferred_element_type=jnp.float32)
+            image = (totals[:, span] + (spread[0:rows] + spread[rows:half])).astype(jnp.bfloat16)
             target[:, span] = image
             if app == 0:
                 fields[1, chunk, mine, :] = image
                 far_copy(1, chunk).start()
                 near_copy(1, chunk).start()
-
-        ahead = min(AHEAD, chunks)
-        for chunk in range(ahead):
-            totals[:, chunk * BLOCK:(chunk + 1) * BLOCK] = inner(chunk)
-        for slot in range(lists):
-            @pl.when(present(slot))
-            def _():
-                flux_wait(app, slot).wait_recv()
-        arrived = jnp.concatenate([in_w[app, slot] for slot in range(lists)], axis=1)
-        for chunk in range(ahead):
-            finish(chunk, totals[:, chunk * BLOCK:(chunk + 1) * BLOCK], arrived)
-        for chunk in range(ahead, chunks):
-            finish(chunk, inner(chunk), arrived)
 
     for app in range(2):
         for chunk in range(chunks):
@@ -291,7 +326,9 @@
         def _():
             weight_copy(slot).wait_send()
             for app in range(2):
-                flux_copy(app, slot).wait_send()
+                for side in range(2):
+                    flux_copy(app, side, slot).wait_send()
+    pair_copy(group).wait_send()
 
 
 def write_out(first_in, second_in, first, second, done):
@@ -326,23 +363,29 @@
             pltpu.VMEM(trans.shape, jnp.float32),
             pltpu.VMEM(face_cells.shape, jnp.int32),
             pltpu.VMEM(send_list.shape, jnp.int32),
-            pltpu.VMEM((cells, 2 * ghosts + face_count), bf16),
+            pltpu.VMEM((coupling.shape[0], 2 * rows, groups * rows), bf16),
+            pltpu.VMEM((coupling.shape[0], groups * rows, 2 * rows), bf16),
+            pltpu.VMEM((cells, ghosts + face_count), bf16),
+            pltpu.VMEM((face_count + ghosts, cells), bf16),
             pltpu.VMEM((ghosts, face_count), bf16),
             pltpu.VMEM((48, face_count), bf16),
             pltpu.VMEM((2, chunks, groups * rows, BLOCK), bf16),
-            pltpu.VMEM((groups * rows, ghosts + face_count), jnp.float32),
+            pltpu.VMEM((2 * rows, face_count), jnp.float32),
+            pltpu.VMEM((groups * rows, face_count), bf16),
             pltpu.VMEM((rows, cells), jnp.float32),
             pltpu.VMEM((2 * rows, face_count), bf16),
-            pltpu.VMEM((2, lists, rows, width), bf16),
-            pltpu.VMEM((2, lists, rows, width), bf16),
+            pltpu.VMEM((2, 2, lists, rows, width), bf16),
+            pltpu.VMEM((2, 2, lists, rows, width), bf16),
             pltpu.VMEM((lists, 16, width), jnp.float32),
             pltpu.VMEM((lists, 16, width), jnp.float32),
             pltpu.VMEM((8, ghosts), jnp.int32),
-            pltpu.SemaphoreType.DMA((chunks + 5,)),
+            pltpu.VMEM((2 * rows, ghosts), bf16),
+            pltpu.SemaphoreType.DMA((chunks + 6,)),
         ]
         + [pltpu.SemaphoreType.DMA((2, chunks))] * 6
-        + [pltpu.SemaphoreType.DMA((2, lists))] * 2
-        + [pltpu.SemaphoreType.DMA((lists,))] * 2,
+        + [pltpu.SemaphoreType.DMA((2, 2, lists))] * 2
+        + [pltpu.SemaphoreType.DMA((lists,))] * 2
+        + [pltpu.SemaphoreType.DMA((1,))] * 2,
         compiler_params=pltpu.CompilerParams(
             collective_id=0, has_side_effects=True, vmem_limit_bytes=61 * 1024 * 1024
         ),

time: 28.3 us -> 26.2 us (0.926)
  Pallas kernels: 27.5 us -> 25.4 us
    pallas_call x1, Pallas kernels: 26.8 us -> 24.7 us  [local(): pl.pallas_call(functools.partial(kernel, parts, groups), out_shape=(pltpu...]
where the time goes in v2:
time: 26.2 us; the launch traced here: 26 us
  Pallas kernels  25.4 us (97%)
  between operations  0.64 us (2%)
    pallas_call x1, Pallas kernels, local(): pl.pallas_call(functools.partial(kernel, parts, groups), out_shape=(pltpu...  24.7 us
    pallas_call x1, Pallas kernels, local(): pl.pallas_call(write_out, out_shape=(image, image), in_specs=[vmem] * 2,...  0.72 us

profile of v2, /device:TPU:0, one launch (start us, length us, event | category | flops | bytes accessed | tf_op | source)
XLA Modules:
  0.0 26.0 jit_solution(15731490964370564333)
XLA Ops:
  0.6 24.7 %shard_map.77 = (bf16[64,1024]{1,0:T(8,128)(2,1)S(1)}, bf16[64,1024]{1,0:T(8,128)(2,1)S(1)}) custom-call(bf16[64,1024]{1,0:T(8,128)(2,1)} %pressure.1, f32[1,1024]{1,0:T(1,128)} %bitcast.1, bf16[11,64,256]{2,1,0:T(8,128)(2,1)} %coupling_in.1, f32[11,3072]{1,0:T(8,128)} %trans_in.1, s32[2,3072]{1,0:T(2,128)} %faces_in.1, s32[1,4,128]{2,1,0:T(4,128)} %sends_in.1), custom_call_target="tpu_custom_call" | custom-call | tf_op jit(solution)/shard_map/pallas_call | solution.py:355
  25.3 0.7 %shard_map.78 = (bf16[64,1024]{1,0:T(8,128)(2,1)}, bf16[64,1024]{1,0:T(8,128)(2,1)}) custom-call(bf16[64,1024]{1,0:T(8,128)(2,1)S(1)} %get-tuple-element.4.first_in, bf16[64,1024]{1,0:T(8,128)(2,1)S(1)} %get-tuple-element.5.second_in), custom_call_target="tpu_custom_call" | custom-call | tf_op jit(solution)/shard_map/pallas_call | solution.py:394

commit v3 on v2

v3 whole, which is shorter than its diff:
```python
import functools

import jax
import jax.numpy as jnp
from jax import lax
from jax.experimental import pallas as pl
from jax.experimental.pallas import tpu as pltpu
from jax.sharding import PartitionSpec as P

MESH = pl.DeviceIdType.MESH
BLOCK = 256
TILE = 512
AHEAD = 1


def onehot(rows, base, index_row, dtype=jnp.bfloat16):
    near = jnp.clip(index_row - base, -1, rows).astype(jnp.float32).astype(jnp.bfloat16)
    iota = lax.broadcasted_iota(jnp.int32, (rows, index_row.shape[1]), 0)
    return iota.astype(jnp.float32).astype(jnp.bfloat16) == near


def kernel(
    parts, groups, pressure, storage_in, coupling_in, trans_in, faces_in, sends_in, first, second,
    storage, coupling, trans, faces, sends, pair, turned,
    wide, tall, ghost_hot, picked_rows, fields, sums, diff, totals, flux, out_w, in_w, slot_weights, slot_owner, fluxes, out_f,
    out_s, in_s, out_t, in_t,
    load, near_send, near_recv, far_send, far_recv, pass_send, pass_recv,
    w_send, w_recv, f_send, f_recv, pair_send, pair_recv, s_send, s_recv,
    t_send, t_recv,
):
    rows, cells = pressure.shape
    terms = coupling.shape[0]
    face_count = faces.shape[1]
    lists, width = sends.shape[1:]
    ghosts = lists * width
    reach = lists // 2
    offsets = list(range(-reach, 0)) + list(range(1, reach + 1))
    chunks = cells // BLOCK
    part = lax.axis_index("cells")
    group = lax.axis_index("modes")
    partner = group + 1 - 2 * lax.rem(group, 2)
    far = lax.rem(group + 2, 4)
    far_partner = lax.rem(partner + 2, 4)

    def band(member):
        return pl.ds(pl.multiple_of(member * rows, rows), rows)

    mine = band(group)
    one = jnp.ones((), jnp.bfloat16)
    zero = jnp.zeros((), jnp.bfloat16)

    def present(slot):
        return jnp.logical_and(part + offsets[slot] >= 0, part + offsets[slot] < parts)

    def band_copy(app, chunk, member, send_sem, recv_sem, target):
        return pltpu.make_async_remote_copy(
            src_ref=fields.at[app, chunk, band(member)],
            dst_ref=fields.at[app, chunk, band(member)],
            send_sem=send_sem.at[app, chunk],
            recv_sem=recv_sem.at[app, chunk],
            device_id={"modes": target},
            device_id_type=MESH,
        )

    def near_copy(app, chunk, member=group):
        return band_copy(app, chunk, member, near_send, near_recv, partner)

    def far_copy(app, chunk, member=group):
        return band_copy(app, chunk, member, far_send, far_recv, far)

    def pass_copy(app, chunk, member=far):
        return band_copy(app, chunk, member, pass_send, pass_recv, partner)

    def ghost_peer(side, slot):
        peer = part + offsets[slot]
        return {"cells": peer} if side == 0 else {"cells": peer, "modes": partner}

    def half_of(member):
        return pl.ds(pl.multiple_of(lax.rem(member, 2) * rows, rows), rows)

    def ghost_copy(side, slot):
        return pltpu.make_async_remote_copy(
            src_ref=out_w.at[slot],
            dst_ref=in_w.at[lists - 1 - slot, half_of(group)],
            send_sem=w_send.at[side, slot],
            recv_sem=w_recv.at[side, lists - 1 - slot],
            device_id=ghost_peer(side, slot),
            device_id_type=MESH,
        )

    def ghost_wait(side, slot):
        return pltpu.make_async_remote_copy(
            src_ref=out_w.at[lists - 1 - slot],
            dst_ref=in_w.at[slot, half_of(group if side == 0 else partner)],
            send_sem=w_send.at[side, lists - 1 - slot],
            recv_sem=w_recv.at[side, slot],
            device_id=ghost_peer(side, slot),
            device_id_type=MESH,
        )

    def flux_copy():
        return pltpu.make_async_remote_copy(
            src_ref=out_f,
            dst_ref=fluxes.at[rows:2 * rows],
            send_sem=f_send.at[0],
            recv_sem=f_recv.at[0],
            device_id={"modes": far},
            device_id_type=MESH,
        )

    def flux_peer(side, slot):
        peer = part + offsets[slot]
        return {"cells": peer} if side == 0 else {"cells": peer, "modes": far}

    def sum_copy(side, slot):
        return pltpu.make_async_remote_copy(
            src_ref=out_s.at[side, slot],
            dst_ref=in_s.at[side, lists - 1 - slot],
            send_sem=s_send.at[side, slot],
            recv_sem=s_recv.at[side, lists - 1 - slot],
            device_id=flux_peer(side, slot),
            device_id_type=MESH,
        )

    def sum_wait(side, slot):
        return pltpu.make_async_remote_copy(
            src_ref=out_s.at[side, lists - 1 - slot],
            dst_ref=in_s.at[side, slot],
            send_sem=s_send.at[side, lists - 1 - slot],
            recv_sem=s_recv.at[side, slot],
            device_id=flux_peer(side, slot),
            device_id_type=MESH,
        )

    def weight_copy(slot):
        return pltpu.make_async_remote_copy(
            src_ref=out_t.at[slot],
            dst_ref=in_t.at[lists - 1 - slot],
            send_sem=t_send.at[slot],
            recv_sem=t_recv.at[lists - 1 - slot],
            device_id={"cells": part + offsets[slot]},
            device_id_type=MESH,
        )

    def weight_wait(slot):
        return pltpu.make_async_remote_copy(
            src_ref=out_t.at[lists - 1 - slot],
            dst_ref=in_t.at[slot],
            send_sem=t_send.at[lists - 1 - slot],
            recv_sem=t_recv.at[slot],
            device_id={"cells": part + offsets[slot]},
            device_id_type=MESH,
        )

    def pair_copy(member):
        return pltpu.make_async_remote_copy(
            src_ref=pair.at[:, half_of(member)],
            dst_ref=pair.at[:, half_of(member)],
            send_sem=pair_send.at[0],
            recv_sem=pair_recv.at[0],
            device_id={"modes": partner},
            device_id_type=MESH,
        )

    def weight_copy(slot):
        return pltpu.make_async_remote_copy(
            src_ref=out_t.at[slot],
            dst_ref=in_t.at[lists - 1 - slot],
            send_sem=t_send.at[slot],
            recv_sem=t_recv.at[lists - 1 - slot],
            device_id={"cells": part + offsets[slot]},
            device_id_type=MESH,
        )

    def weight_wait(slot):
        return pltpu.make_async_remote_copy(
            src_ref=out_t.at[lists - 1 - slot],
            dst_ref=in_t.at[slot],
            send_sem=t_send.at[lists - 1 - slot],
            recv_sem=t_recv.at[slot],
            device_id={"cells": part + offsets[slot]},
            device_id_type=MESH,
        )

    loads = []
    for index, (source, target) in enumerate(
        [(faces_in, faces), (trans_in, trans), (sends_in, sends)]
        + [
            (pressure.at[:, chunk * BLOCK:(chunk + 1) * BLOCK], fields.at[0, chunk, mine])
            for chunk in range(chunks)
        ]
        + [(coupling_in, pair.at[:, half_of(group)]), (coupling_in, coupling), (storage_in, storage)]
    ):
        loads.append(pltpu.make_async_copy(source, target, load.at[index]))
    for copy in loads:
        copy.start()
    in_w[...] = jnp.zeros_like(in_w)
    in_s[...] = jnp.zeros_like(in_s)
    in_t[...] = jnp.zeros_like(in_t)
    barrier = pltpu.get_barrier_semaphore()
    for peer in (partner, far):
        pl.semaphore_signal(barrier, inc=1, device_id={"modes": peer}, device_id_type=MESH)
    peers = 2
    for slot in range(lists):
        peers = peers + 3 * present(slot).astype(jnp.int32)

        @pl.when(present(slot))
        def _():
            pl.semaphore_signal(
                barrier, inc=1, device_id={"cells": part + offsets[slot]}, device_id_type=MESH
            )
            for peer in (partner, far):
                pl.semaphore_signal(
                    barrier, inc=1, device_id={"cells": part + offsets[slot], "modes": peer}, device_id_type=MESH
                )
    def build_sends(base):
        for slot in range(lists):
            hot = onehot(BLOCK, base, sends[0, slot:slot + 1])
            wide[base:base + BLOCK, slot * width:(slot + 1) * width] = jnp.where(hot, one, zero)

    half = 2 * rows
    near_half = pl.ds(pl.multiple_of(lax.div(group, 2) * half, half), half)
    far_half = pl.ds(pl.multiple_of((1 - lax.div(group, 2)) * half, half), half)

    def build_faces(index, carry):
        at = pl.ds(pl.multiple_of(index * TILE, TILE), TILE)
        to = pl.ds(pl.multiple_of(ghosts + index * TILE, TILE), TILE)
        for chunk in range(chunks):
            base = chunk * BLOCK
            plus = onehot(BLOCK, base, faces[0:1, at])
            minus = onehot(BLOCK, base, faces[1:2, at])
            signs = jnp.where(plus, one, jnp.where(minus, -one, zero))
            wide[base:base + BLOCK, to] = signs
            tall[at, base:base + BLOCK] = signs.T
            part_sum = jnp.dot(fields[0, chunk, near_half], signs, preferred_element_type=jnp.float32)
            total = part_sum if chunk == 0 else total + part_sum
        diff[near_half, at] = total.astype(jnp.bfloat16)
        return carry

    def build_ghost(index, carry):
        at = pl.ds(pl.multiple_of(index * TILE, TILE), TILE)
        other = faces[1:2, at]
        for base in range(0, ghosts, BLOCK):
            hot = onehot(BLOCK, cells + base, other)
            ghost_hot[base:base + BLOCK, at] = jnp.where(hot, one, zero)
        return carry

    def find_slots():
        t = trans[...]
        t_high = t.astype(jnp.bfloat16)
        t_low = (t - t_high.astype(jnp.float32)).astype(jnp.bfloat16)
        picked_rows[...] = jnp.zeros_like(picked_rows)
        picked_rows[0:terms] = t_high
        picked_rows[16:16 + terms] = t_low
        owner_next = faces[0:1] + 1
        picked_rows[32:33] = (owner_next // 32).astype(jnp.float32).astype(jnp.bfloat16)
        picked_rows[33:34] = (owner_next % 32).astype(jnp.float32).astype(jnp.bfloat16)
        lax.fori_loop(0, face_count // TILE, build_ghost, 0)
        found = lax.dot_general(
            picked_rows[...], ghost_hot[...], (((1,), (1,)), ((), ())), preferred_element_type=jnp.float32
        )
        slot_weights[...] = found[0:16] + found[16:32]
        slot_owner[0:1] = (found[32:33] * 32.0 + found[33:34] - 1.0).astype(jnp.int32)
        for slot in range(lists):
            out_t[slot] = slot_weights[:, slot * width:(slot + 1) * width]

    def build_owners():
        for base in range(0, cells, BLOCK):
            hot = onehot(BLOCK, base, slot_owner[0:1])
            tall[face_count:, base:base + BLOCK] = jnp.where(hot, -one, zero).T

    def differ(app, chunk, members):
        rows_of = slice(chunk * BLOCK, (chunk + 1) * BLOCK)
        field = fields[app, chunk, members]
        for start in range(0, face_count, TILE):
            at = slice(start, start + TILE)
            total = jnp.dot(
                field, wide[rows_of, ghosts + start:ghosts + start + TILE], preferred_element_type=jnp.float32
            )
            if chunk > 0:
                total += sums[:, at]
            if chunk < chunks - 1:
                sums[:, at] = total
            else:
                diff[members, at] = total.astype(jnp.bfloat16)

    def pick(app, members):
        total = jnp.dot(fields[app, 0, members], wide[0:BLOCK, 0:ghosts], preferred_element_type=jnp.float32)
        for chunk in range(1, chunks):
            total += jnp.dot(
                fields[app, chunk, members], wide[chunk * BLOCK:(chunk + 1) * BLOCK, 0:ghosts],
                preferred_element_type=jnp.float32,
            )
        return total.astype(jnp.bfloat16)

    def send_ghosts():
        total = pick(0, mine)
        for slot in range(lists):
            out_w[slot] = total[:, slot * width:(slot + 1) * width]

            @pl.when(present(slot))
            def _():
                for side in range(2):
                    ghost_copy(side, slot).start()

    def send_sums():
        ghost = pick(1, near_half)
        for slot in range(lists):
            @pl.when(present(slot))
            def _():
                weight_wait(slot).wait_recv()
        weights = jnp.concatenate([in_t[slot] for slot in range(lists)], axis=1)
        for side, member in ((1, far), (0, group)):
            sent = mix(turned[:, band(member)].reshape(terms * rows, half), ghost, weights)
            for slot in range(lists):
                out_s[side, slot] = sent[:, slot * width:(slot + 1) * width].astype(jnp.bfloat16)

                @pl.when(present(slot))
                def _():
                    sum_copy(side, slot).start()

    def mix_ghosts():
        for slot in range(lists):
            @pl.when(present(slot))
            def _():
                for side in range(2):
                    ghost_wait(side, slot).wait_recv()
        ghost = jnp.concatenate([in_w[slot] for slot in range(lists)], axis=1)
        for member in (far, group):
            sent = mix(turned[:, band(member)].reshape(terms * rows, half), ghost, slot_weights[...])
            if member is far:
                out_f[...] = sent.astype(jnp.bfloat16)
                flux_copy().start()
            else:
                fluxes[0:rows] = sent.astype(jnp.bfloat16)

    def pass_on(app, chunk):
        far_copy(app, chunk, far).wait_recv()
        pass_copy(app, chunk).start()

    def mix(stacked, column, weights):
        mixed = jnp.dot(stacked, column, preferred_element_type=jnp.float32)
        total = mixed[0:rows] * weights[0:1]
        for term in range(1, terms):
            total += mixed[term * rows:(term + 1) * rows] * weights[term:term + 1]
        return total

    for copy in loads[:3]:
        copy.wait()
    find_slots()
    for chunk in range(chunks):
        build_sends(chunk * BLOCK)
    for copy in loads[3:]:
        copy.wait()
    pl.semaphore_wait(barrier, peers)
    for chunk in range(chunks):
        far_copy(0, chunk).start()
        near_copy(0, chunk).start()
    send_ghosts()
    pair_copy(group).start()
    for slot in range(lists):
        @pl.when(present(slot))
        def _():
            weight_copy(slot).start()
    for chunk in range(chunks):
        near_copy(0, chunk, partner).wait_recv()
    lax.fori_loop(0, face_count // TILE, build_faces, 0)
    pair_copy(partner).wait_recv()
    for term in range(terms):
        turned[term] = pair[term].T
    for app, target in enumerate((first, second)):
        if app == 1:
            for chunk in range(chunks):
                near_copy(app, chunk, partner).wait_recv()
            send_sums()
        for chunk in range(chunks):
            pass_on(app, chunk)
            if app == 1:
                differ(app, chunk, near_half)
        if app == 0:
            mix_ghosts()
            build_owners()
        for chunk in range(chunks):
            pass_copy(app, chunk, far_partner).wait_recv()
            differ(app, chunk, far_half)

        stacked = coupling[...].reshape(terms * rows, groups * rows)
        for start in range(0, face_count, TILE):
            at = slice(start, start + TILE)
            total = mix(stacked, diff[:, at], trans[:, at])
            high = total.astype(jnp.bfloat16)
            flux[0:rows, at] = high
            flux[rows:2 * rows, at] = (total - high.astype(jnp.float32)).astype(jnp.bfloat16)

        def inner(chunk):
            span = slice(chunk * BLOCK, (chunk + 1) * BLOCK)
            spread = jnp.dot(flux[...], tall[0:face_count, span], preferred_element_type=jnp.float32)
            image = storage[:, span] * fields[app, chunk, mine, :].astype(jnp.float32)
            totals[:, span] = image + spread[0:rows] + spread[rows:2 * rows]

        def finish(chunk):
            span = slice(chunk * BLOCK, (chunk + 1) * BLOCK)
            spread = jnp.dot(arrived, tall[face_count:, span], preferred_element_type=jnp.float32)
            image = (totals[:, span] + (spread[0:rows] + spread[rows:half])).astype(jnp.bfloat16)
            target[:, span] = image
            if app == 0:
                fields[1, chunk, mine, :] = image
                far_copy(1, chunk).start()
                near_copy(1, chunk).start()

        for chunk in range(AHEAD):
            inner(chunk)
        if app == 0:
            flux_copy().wait_recv()
            arrived = fluxes[...]
        else:
            for slot in range(lists):
                @pl.when(present(slot))
                def _():
                    for side in range(2):
                        sum_wait(side, slot).wait_recv()
            arrived = jnp.concatenate(
                [jnp.concatenate([in_s[side, slot] for slot in range(lists)], axis=1) for side in range(2)], axis=0
            )
        for chunk in range(chunks):
            if chunk >= AHEAD:
                inner(chunk)
            finish(chunk)

    for app in range(2):
        for chunk in range(chunks):
            far_copy(app, chunk).wait_send()
            near_copy(app, chunk).wait_send()
            pass_copy(app, chunk).wait_send()
    flux_copy().wait_send()
    for slot in range(lists):
        @pl.when(present(slot))
        def _():
            weight_copy(slot).wait_send()
            for side in range(2):
                ghost_copy(side, slot).wait_send()
                sum_copy(side, slot).wait_send()
    pair_copy(group).wait_send()


def write_out(first_in, second_in, first, second, done):
    copies = [
        pltpu.make_async_copy(source, target, done.at[index])
        for index, (source, target) in enumerate(((first_in, first), (second_in, second)))
    ]
    for copy in copies:
        copy.start()
    for copy in copies:
        copy.wait()


def local(parts, groups, pressure, storage, coupling, trans, face_cells, send_list):
    assert groups == 4
    rows, cells = pressure.shape
    face_count = face_cells.shape[1]
    lists, width = send_list.shape[1:]
    ghosts = lists * width
    chunks = cells // BLOCK
    bf16 = jnp.bfloat16
    vmem = pl.BlockSpec(memory_space=pltpu.VMEM)
    image = jax.ShapeDtypeStruct((rows, cells), bf16)
    images = pl.pallas_call(
        functools.partial(kernel, parts, groups),
        out_shape=(pltpu.VMEM((rows, cells), bf16), pltpu.VMEM((rows, cells), bf16)),
        in_specs=[pl.BlockSpec(memory_space=pltpu.HBM)] * 6,
        out_specs=(vmem, vmem),
        scratch_shapes=[
            pltpu.VMEM((1, cells), jnp.float32),
            pltpu.VMEM(coupling.shape, bf16),
            pltpu.VMEM(trans.shape, jnp.float32),
            pltpu.VMEM(face_cells.shape, jnp.int32),
            pltpu.VMEM(send_list.shape, jnp.int32),
            pltpu.VMEM((coupling.shape[0], 2 * rows, groups * rows), bf16),
            pltpu.VMEM((coupling.shape[0], groups * rows, 2 * rows), bf16),
            pltpu.VMEM((cells, ghosts + face_count), bf16),
            pltpu.VMEM((face_count + ghosts, cells), bf16),
            pltpu.VMEM((ghosts, face_count), bf16),
            pltpu.VMEM((48, face_count), bf16),
            pltpu.VMEM((2, chunks, groups * rows, BLOCK), bf16),
            pltpu.VMEM((2 * rows, face_count), jnp.float32),
            pltpu.VMEM((groups * rows, face_count), bf16),
            pltpu.VMEM((rows, cells), jnp.float32),
            pltpu.VMEM((2 * rows, face_count), bf16),
            pltpu.VMEM((lists, rows, width), bf16),
            pltpu.VMEM((lists, 2 * rows, width), bf16),
            pltpu.VMEM((16, ghosts), jnp.float32),
            pltpu.VMEM((8, ghosts), jnp.int32),
            pltpu.VMEM((2 * rows, ghosts), bf16),
            pltpu.VMEM((rows, ghosts), bf16),
            pltpu.VMEM((2, lists, rows, width), bf16),
            pltpu.VMEM((2, lists, rows, width), bf16),
            pltpu.VMEM((lists, 16, width), jnp.float32),
            pltpu.VMEM((lists, 16, width), jnp.float32),
            pltpu.SemaphoreType.DMA((chunks + 6,)),
        ]
        + [pltpu.SemaphoreType.DMA((2, chunks))] * 6
        + [pltpu.SemaphoreType.DMA((2, lists))] * 2
        + [pltpu.SemaphoreType.DMA((1,))] * 4
        + [pltpu.SemaphoreType.DMA((2, lists))] * 2
        + [pltpu.SemaphoreType.DMA((lists,))] * 2,
        compiler_params=pltpu.CompilerParams(
            collective_id=0, has_side_effects=True, vmem_limit_bytes=61 * 1024 * 1024
        ),
    )(pressure, storage.reshape(1, cells), coupling, trans, face_cells, send_list)
    hbm = pl.BlockSpec(memory_space=pltpu.HBM)
    return pl.pallas_call(
        write_out,
        out_shape=(image, image),
        in_specs=[vmem] * 2,
        out_specs=(hbm, hbm),
        scratch_shapes=[pltpu.SemaphoreType.DMA((2,))],
        compiler_params=pltpu.CompilerParams(vmem_limit_bytes=1024 * 1024),
    )(*images)


def solution(mesh):
    placed = (
        P("modes", "cells"),
        P("cells"),
        P(None, "modes", None),
        P(None, "cells"),
        P(None, "cells"),
        P("cells", None, None),
    )
    return jax.shard_map(
        functools.partial(local, mesh.shape["cells"], mesh.shape["modes"]),
        mesh=mesh,
        in_specs=placed,
        out_specs=(P("modes", "cells"), P("modes", "cells")),
        check_vma=False,
    )
```

time: 26.2 us -> 24.5 us (0.935)
  Pallas kernels: 25.4 us -> 23.7 us
    pallas_call x1, Pallas kernels: 24.7 us -> 22.9 us  [local(): pl.pallas_call(functools.partial(kernel, parts, groups), out_shape=(pltpu...]
where the time goes in v3:
time: 24.5 us; the launch traced here: 24.3 us
  Pallas kernels  23.7 us (97%)
  between operations  0.64 us (3%)
    pallas_call x1, Pallas kernels, local(): pl.pallas_call(functools.partial(kernel, parts, groups), out_shape=(pltpu...  22.9 us
    pallas_call x1, Pallas kernels, local(): pl.pallas_call(write_out, out_shape=(image, image), in_specs=[vmem] * 2,...  0.72 us

profile of v3, /device:TPU:0, one launch (start us, length us, event | category | flops | bytes accessed | tf_op | source)
XLA Modules:
  0.0 24.3 jit_solution(9949449839941197584)
XLA Ops:
  0.6 22.9 %shard_map.77 = (bf16[64,1024]{1,0:T(8,128)(2,1)S(1)}, bf16[64,1024]{1,0:T(8,128)(2,1)S(1)}) custom-call(bf16[64,1024]{1,0:T(8,128)(2,1)} %pressure.1, f32[1,1024]{1,0:T(1,128)} %bitcast.1, bf16[11,64,256]{2,1,0:T(8,128)(2,1)} %coupling_in.1, f32[11,3072]{1,0:T(8,128)} %trans_in.1, s32[2,3072]{1,0:T(2,128)} %faces_in.1, s32[1,4,128]{2,1,0:T(4,128)} %sends_in.1), custom_call_target="tpu_custom_call" | custom-call | tf_op jit(solution)/shard_map/pallas_call | solution.py:467
  23.6 0.7 %shard_map.78 = (bf16[64,1024]{1,0:T(8,128)(2,1)}, bf16[64,1024]{1,0:T(8,128)(2,1)}) custom-call(bf16[64,1024]{1,0:T(8,128)(2,1)S(1)} %get-tuple-element.4.first_in, bf16[64,1024]{1,0:T(8,128)(2,1)S(1)} %get-tuple-element.5.second_in), custom_call_target="tpu_custom_call" | custom-call | tf_op jit(solution)/shard_map/pallas_call | solution.py:511

commit v4 on v3

--- a/solution.py
+++ b/solution.py
@@ -256,6 +256,8 @@
         picked_rows[32:33] = (owner_next // 32).astype(jnp.float32).astype(jnp.bfloat16)
         picked_rows[33:34] = (owner_next % 32).astype(jnp.float32).astype(jnp.bfloat16)
         lax.fori_loop(0, face_count // TILE, build_ghost, 0)
+
+    def weigh_slots():
         found = lax.dot_general(
             picked_rows[...], ghost_hot[...], (((1,), (1,)), ((), ())), preferred_element_type=jnp.float32
         )
@@ -348,26 +350,27 @@
     for copy in loads[:3]:
         copy.wait()
     find_slots()
-    for chunk in range(chunks):
-        build_sends(chunk * BLOCK)
     for copy in loads[3:]:
         copy.wait()
     pl.semaphore_wait(barrier, peers)
     for chunk in range(chunks):
         far_copy(0, chunk).start()
         near_copy(0, chunk).start()
+    pair_copy(group).start()
+    for chunk in range(chunks):
+        build_sends(chunk * BLOCK)
     send_ghosts()
-    pair_copy(group).start()
+    for chunk in range(chunks):
+        near_copy(0, chunk, partner).wait_recv()
+    lax.fori_loop(0, face_count // TILE, build_faces, 0, unroll=True)
+    pair_copy(partner).wait_recv()
+    for term in range(terms):
+        turned[term] = pair[term].T
+    weigh_slots()
     for slot in range(lists):
         @pl.when(present(slot))
         def _():
             weight_copy(slot).start()
-    for chunk in range(chunks):
-        near_copy(0, chunk, partner).wait_recv()
-    lax.fori_loop(0, face_count // TILE, build_faces, 0)
-    pair_copy(partner).wait_recv()
-    for term in range(terms):
-        turned[term] = pair[term].T
     for app, target in enumerate((first, second)):
         if app == 1:
             for chunk in range(chunks):
@@ -393,9 +396,10 @@
             flux[rows:2 * rows, at] = (total - high.astype(jnp.float32)).astype(jnp.bfloat16)
 
         def inner(chunk):
-            span = slice(chunk * BLOCK, (chunk + 1) * BLOCK)
+            span = slice(chunk * BLOCK, (chunk + 2) * BLOCK)
             spread = jnp.dot(flux[...], tall[0:face_count, span], preferred_element_type=jnp.float32)
-            image = storage[:, span] * fields[app, chunk, mine, :].astype(jnp.float32)
+            own = jnp.concatenate([fields[app, chunk, mine], fields[app, chunk + 1, mine]], axis=1)
+            image = storage[:, span] * own.astype(jnp.float32)
             totals[:, span] = image + spread[0:rows] + spread[rows:2 * rows]
 
         def finish(chunk):
@@ -408,8 +412,7 @@
                 far_copy(1, chunk).start()
                 near_copy(1, chunk).start()
 
-        for chunk in range(AHEAD):
-            inner(chunk)
+        inner(0)
         if app == 0:
             flux_copy().wait_recv()
             arrived = fluxes[...]
@@ -423,7 +426,7 @@
                 [jnp.concatenate([in_s[side, slot] for slot in range(lists)], axis=1) for side in range(2)], axis=0
             )
         for chunk in range(chunks):
-            if chunk >= AHEAD:
+            if chunk > 0 and chunk % 2 == 0:
                 inner(chunk)
             finish(chunk)
 

time: 24.5 us -> 23.6 us (0.963)
  Pallas kernels: 23.7 us -> 22.8 us
    pallas_call x1, Pallas kernels: 22.9 us -> 22.1 us  [local(): pl.pallas_call(functools.partial(kernel, parts, groups), out_shape=(pltpu...]
where the time goes in v4:
time: 23.6 us; the launch traced here: 23.5 us
  Pallas kernels  22.8 us (97%)
  between operations  0.64 us (3%)
    pallas_call x1, Pallas kernels, local(): pl.pallas_call(functools.partial(kernel, parts, groups), out_shape=(pltpu...  22.1 us
    pallas_call x1, Pallas kernels, local(): pl.pallas_call(write_out, out_shape=(image, image), in_specs=[vmem] * 2,...  0.72 us

profile of v4, /device:TPU:0, one launch (start us, length us, event | category | flops | bytes accessed | tf_op | source)
XLA Modules:
  0.0 23.5 jit_solution(3616902332871693971)
XLA Ops:
  0.6 22.1 %shard_map.77 = (bf16[64,1024]{1,0:T(8,128)(2,1)S(1)}, bf16[64,1024]{1,0:T(8,128)(2,1)S(1)}) custom-call(bf16[64,1024]{1,0:T(8,128)(2,1)} %pressure.1, f32[1,1024]{1,0:T(1,128)} %bitcast.1, bf16[11,64,256]{2,1,0:T(8,128)(2,1)} %coupling_in.1, f32[11,3072]{1,0:T(8,128)} %trans_in.1, s32[2,3072]{1,0:T(2,128)} %faces_in.1, s32[1,4,128]{2,1,0:T(4,128)} %sends_in.1), custom_call_target="tpu_custom_call" | custom-call | tf_op jit(solution)/shard_map/pallas_call | solution.py:470
  22.7 0.7 %shard_map.78 = (bf16[64,1024]{1,0:T(8,128)(2,1)}, bf16[64,1024]{1,0:T(8,128)(2,1)}) custom-call(bf16[64,1024]{1,0:T(8,128)(2,1)S(1)} %get-tuple-element.4.first_in, bf16[64,1024]{1,0:T(8,128)(2,1)S(1)} %get-tuple-element.5.second_in), custom_call_target="tpu_custom_call" | custom-call | tf_op jit(solution)/shard_map/pallas_call | solution.py:514

commit v5 on v4

--- a/solution.py
+++ b/solution.py
@@ -10,7 +10,7 @@
 MESH = pl.DeviceIdType.MESH
 BLOCK = 256
 TILE = 512
-AHEAD = 1
+WIDE = 1536
 
 
 def onehot(rows, base, index_row, dtype=jnp.bfloat16):
@@ -274,10 +274,10 @@
     def differ(app, chunk, members):
         rows_of = slice(chunk * BLOCK, (chunk + 1) * BLOCK)
         field = fields[app, chunk, members]
-        for start in range(0, face_count, TILE):
-            at = slice(start, start + TILE)
+        for start in range(0, face_count, WIDE):
+            at = slice(start, start + WIDE)
             total = jnp.dot(
-                field, wide[rows_of, ghosts + start:ghosts + start + TILE], preferred_element_type=jnp.float32
+                field, wide[rows_of, ghosts + start:ghosts + start + WIDE], preferred_element_type=jnp.float32
             )
             if chunk > 0:
                 total += sums[:, at]
@@ -360,17 +360,17 @@
     for chunk in range(chunks):
         build_sends(chunk * BLOCK)
     send_ghosts()
+    weigh_slots()
+    for slot in range(lists):
+        @pl.when(present(slot))
+        def _():
+            weight_copy(slot).start()
     for chunk in range(chunks):
         near_copy(0, chunk, partner).wait_recv()
     lax.fori_loop(0, face_count // TILE, build_faces, 0, unroll=True)
     pair_copy(partner).wait_recv()
     for term in range(terms):
         turned[term] = pair[term].T
-    weigh_slots()
-    for slot in range(lists):
-        @pl.when(present(slot))
-        def _():
-            weight_copy(slot).start()
     for app, target in enumerate((first, second)):
         if app == 1:
             for chunk in range(chunks):

time: 23.6 us -> 23 us (0.975)
  Pallas kernels: 22.8 us -> 22.2 us
    pallas_call x1, Pallas kernels: 22.1 us -> 21.5 us  [local(): pl.pallas_call(functools.partial(kernel, parts, groups), out_shape=(pltpu...]
where the time goes in v5:
time: 23 us; the launch traced here: 22.9 us
  Pallas kernels  22.2 us (97%)
  between operations  0.64 us (3%)
    pallas_call x1, Pallas kernels, local(): pl.pallas_call(functools.partial(kernel, parts, groups), out_shape=(pltpu...  21.5 us
    pallas_call x1, Pallas kernels, local(): pl.pallas_call(write_out, out_shape=(image, image), in_specs=[vmem] * 2,...  0.72 us

profile of v5, /device:TPU:0, one launch (start us, length us, event | category | flops | bytes accessed | tf_op | source)
XLA Modules:
  0.0 22.9 jit_solution(1872362377610946071)
XLA Ops:
  0.6 21.5 %shard_map.77 = (bf16[64,1024]{1,0:T(8,128)(2,1)S(1)}, bf16[64,1024]{1,0:T(8,128)(2,1)S(1)}) custom-call(bf16[64,1024]{1,0:T(8,128)(2,1)} %pressure.1, f32[1,1024]{1,0:T(1,128)} %bitcast.1, bf16[11,64,256]{2,1,0:T(8,128)(2,1)} %coupling_in.1, f32[11,3072]{1,0:T(8,128)} %trans_in.1, s32[2,3072]{1,0:T(2,128)} %faces_in.1, s32[1,4,128]{2,1,0:T(4,128)} %sends_in.1), custom_call_target="tpu_custom_call" | custom-call | tf_op jit(solution)/shard_map/pallas_call | solution.py:470
  22.2 0.7 %shard_map.78 = (bf16[64,1024]{1,0:T(8,128)(2,1)}, bf16[64,1024]{1,0:T(8,128)(2,1)}) custom-call(bf16[64,1024]{1,0:T(8,128)(2,1)S(1)} %get-tuple-element.4.first_in, bf16[64,1024]{1,0:T(8,128)(2,1)S(1)} %get-tuple-element.5.second_in), custom_call_target="tpu_custom_call" | custom-call | tf_op jit(solution)/shard_map/pallas_call | solution.py:514

commit v6 on v5

--- a/solution.py
+++ b/solution.py
@@ -388,8 +388,8 @@
             differ(app, chunk, far_half)
 
         stacked = coupling[...].reshape(terms * rows, groups * rows)
-        for start in range(0, face_count, TILE):
-            at = slice(start, start + TILE)
+        for start in range(0, face_count, WIDE):
+            at = slice(start, start + WIDE)
             total = mix(stacked, diff[:, at], trans[:, at])
             high = total.astype(jnp.bfloat16)
             flux[0:rows, at] = high

time: 23 us -> 23 us (level)
  no operation moved by 1% of the time
where the time goes in v6:
time: 23 us; the launch traced here: 22.9 us
  Pallas kernels  22.2 us (97%)
  between operations  0.64 us (3%)
    pallas_call x1, Pallas kernels, local(): pl.pallas_call(functools.partial(kernel, parts, groups), out_shape=(pltpu...  21.5 us
    pallas_call x1, Pallas kernels, local(): pl.pallas_call(write_out, out_shape=(image, image), in_specs=[vmem] * 2,...  0.72 us

profile of v6, /device:TPU:0, one launch (start us, length us, event | category | flops | bytes accessed | tf_op | source)
XLA Modules:
  0.0 22.9 jit_solution(1872362377610946071)
XLA Ops:
  0.6 21.5 %shard_map.77 = (bf16[64,1024]{1,0:T(8,128)(2,1)S(1)}, bf16[64,1024]{1,0:T(8,128)(2,1)S(1)}) custom-call(bf16[64,1024]{1,0:T(8,128)(2,1)} %pressure.1, f32[1,1024]{1,0:T(1,128)} %bitcast.1, bf16[11,64,256]{2,1,0:T(8,128)(2,1)} %coupling_in.1, f32[11,3072]{1,0:T(8,128)} %trans_in.1, s32[2,3072]{1,0:T(2,128)} %faces_in.1, s32[1,4,128]{2,1,0:T(4,128)} %sends_in.1), custom_call_target="tpu_custom_call" | custom-call | tf_op jit(solution)/shard_map/pallas_call | solution.py:470
  22.2 0.7 %shard_map.78 = (bf16[64,1024]{1,0:T(8,128)(2,1)}, bf16[64,1024]{1,0:T(8,128)(2,1)}) custom-call(bf16[64,1024]{1,0:T(8,128)(2,1)S(1)} %get-tuple-element.4.first_in, bf16[64,1024]{1,0:T(8,128)(2,1)S(1)} %get-tuple-element.5.second_in), custom_call_target="tpu_custom_call" | custom-call | tf_op jit(solution)/shard_map/pallas_call | solution.py:514
